TPU v7x, 128 devices: a whole 4x4x4 slice. The times are simulated.
128 devices in a mesh: prow: 8 (over x_lo, z), pcol: 16 (over y, x_hi, core).
Axes of the slice: x: 4 (x_hi: 2, x_lo: 2; x = x_hi * 2 + x_lo), y: 4, z: 4, core: 2. Of those that a mesh axis runs over, the one named last changes fastest.
Arguments:
- values: float32 [12, 8, 4, 16, 256, 256], P(None, 'prow', None, 'pcol'), may hold values from -6 to 6
- pattern: int32 [12, 8, 4, 16], P(None, 'prow', None, 'pcol'), may hold values from 0 to 1
Outputs:
- factored: float32 [12, 8, 4, 16, 256, 256], P(None, 'prow', None, 'pcol')
All inputs are finite; a program needn't handle non-finite values.
Results may differ from a plain program's by a relative error of at most 0.0003.
Values sent between devices are 32-bit elements; how exact they have to be, the bound alone decides.
A program may use at most 128 MiB of HBM per device.

v0:
```python
import math
import jax
import jax.numpy as jnp
from jax import lax
from jax.sharding import Mesh
from jax.sharding import PartitionSpec as P

SWEEPS = 3
PROW = ("prow_0", "prow_1")
shift_coef = 5.0


def picked(value, axis, root):
    return lax.dynamic_index_in_dim(lax.all_gather(value, axis), root, 0, keepdims=False)


def rows_for(lines, peers):
    spare = -lines.shape[0] % peers
    if not spare:
        return lines
    return jnp.concatenate([lines, jnp.zeros((spare, *lines.shape[1:]), lines.dtype)])


def spread(value, axis, root):
    lines = jnp.where(lax.axis_index(axis) == root, value, jnp.zeros_like(value)).reshape(
        -1, *value.shape[1:][-1:]
    )
    padded = rows_for(lines, lax.axis_size(axis))
    own = lax.psum_scatter(padded, axis, scatter_dimension=0, tiled=True)
    return lax.all_gather(own, axis, axis=0, tiled=True)[: len(lines)].reshape(value.shape)


def broadcast_by_axis(value, axes, root):
    value = jnp.where(lax.axis_index(axes) == root, value, jnp.zeros_like(value))
    for axis in axes:
        value = lax.psum(value, axis)
    return value


def newton(block, shift):
    width = block.shape[0]
    eye = jnp.eye(width, dtype=jnp.float32)
    approx = eye / shift
    for step in range(SWEEPS):
        inner = jnp.dot(block, approx, precision=lax.Precision.HIGHEST)
        approx = jnp.dot(approx, 2.0 * eye - inner, precision=lax.Precision.HIGHEST)
    return approx


def spread_inverse(block, shift, root_row):
    return picked(newton(block, shift), PROW, root_row)


def apply_panel(blocks, rows_g, cols_g, mult, upper, k):
    product = jnp.einsum("rab,cbe->rcae", mult, upper, precision=lax.Precision.HIGHEST)
    below = rows_g > k
    trail = (below[:, None] & (cols_g > k)[None, :])[:, :, None, None]
    store = (below[:, None] & (cols_g == k)[None, :])[:, :, None, None]
    out = jnp.where(trail, blocks - product, blocks)
    return jnp.where(store, mult[:, None], out)


def drop_one(array, index, axis_pos):
    return jnp.concatenate(
        [
            lax.slice_in_dim(array, 0, index, axis=axis_pos),
            lax.slice_in_dim(array, index + 1, array.shape[axis_pos], axis=axis_pos),
        ],
        axis=axis_pos,
    )


def put_one(array, piece, index, axis_pos):
    return jnp.concatenate(
        [lax.slice_in_dim(array, 0, index, axis=axis_pos), piece, array], axis=axis_pos
    )


def factor_panel(column, row, k, shift, nprow, npcol):
    root_row, loc_row = (k % nprow, k // nprow)
    root_col = k % npcol
    column = spread(column, "pcol", root_col)
    inverse = spread_inverse(column[loc_row], shift, root_row)
    mult = jnp.einsum("rab,be->rae", column, inverse, precision=lax.Precision.HIGHEST)
    upper = broadcast_by_axis(row, PROW, root_row)
    return (mult, upper)


def body(values, pattern):
    rows_loc, cols_loc, width = (values.shape[0], values.shape[2], values.shape[4])
    nprow = lax.axis_size(PROW)
    npcol = lax.axis_size("pcol")
    rows_g = jnp.arange(rows_loc, dtype=jnp.int32) * nprow + lax.axis_index(PROW)
    cols_g = jnp.arange(cols_loc, dtype=jnp.int32) * npcol + lax.axis_index("pcol")
    shift = shift_coef * math.sqrt(width)
    eye = jnp.eye(width, dtype=jnp.float32)
    blocks = values[:, 0, :, 0] * pattern[:, 0, :, 0].astype(jnp.float32)[:, :, None, None]
    diag = jnp.where(rows_g[:, None] == cols_g[None, :], shift, 0.0).astype(jnp.float32)
    blocks = blocks + diag[:, :, None, None] * eye
    row_first, col_first = (0 // nprow, 0 // npcol)
    row_next, col_next = (1 // nprow, 1 // npcol)
    mult_first, upper_first = factor_panel(
        blocks[:, col_first], blocks[row_first], 0, shift, nprow, npcol
    )
    column = apply_panel(
        blocks[:, col_next : col_next + 1],
        rows_g,
        cols_g[col_next : col_next + 1],
        mult_first,
        upper_first[col_next : col_next + 1],
        0,
    )[:, 0]
    row = apply_panel(
        blocks[row_next : row_next + 1],
        rows_g[row_next : row_next + 1],
        cols_g,
        mult_first[row_next : row_next + 1],
        upper_first,
        0,
    )[0]
    mult_next, upper_next = factor_panel(column, row, 1, shift, nprow, npcol)
    inner = drop_one(drop_one(blocks, row_next, 0), col_next, 1)
    inner = apply_panel(
        inner,
        drop_one(rows_g, row_next, 0),
        drop_one(cols_g, col_next, 0),
        drop_one(mult_first, row_next, 0),
        drop_one(upper_first, col_next, 0),
        0,
    )
    inner = put_one(inner, drop_one(column, row_next, 0)[:, None], col_next, 1)
    blocks = put_one(inner, row[None], row_next, 0)
    blocks = apply_panel(blocks, rows_g, cols_g, mult_next, upper_next, 1)
    return blocks[:, None, :, None]


def solution(mesh):
    torus = Mesh(mesh.devices.reshape(2, 4, mesh.shape["pcol"]), ("prow_0", "prow_1", "pcol"))
    return jax.shard_map(
        body,
        mesh=torus,
        in_specs=(P(None, PROW, None, "pcol", None, None), P(None, PROW, None, "pcol")),
        out_specs=P(None, PROW, None, "pcol", None, None),
        check_vma=False,
    )
```

profile of v0, /device:TPU:0, one launch (start us, length us, event | category | flops | bytes accessed | tf_op | source)
XLA Modules:
  0.0 466.2 jit_solution(778879318605547930)
XLA Ops:
  7.4 0.7 convert_element_type.19
  8.1 0.1 compare_select_fusion
  8.2 12.2 %fusion.2 = f32[12,4,256,256]{3,2,0,1:T(8,128)} fusion(f32[12,1,4,1,256,256]{5,4,3,2,1,0:T(8,128)} %param.2, f32[256,256]{1,0:T(8,128)S(1)} %fusion.18, f32[12,4]{0,1:T(4,128)S(1)} %compare_select_fusion, f32[12,4]{0,1:T(4,128)S(1)} %bitcast.93), kind=kLoop, calls=%fused_computation.5 | loop fusion | flops 9437184 | bytes 25428352 | tf_op jit(solution)/shard_map/add | solution.py:99
  20.4 3.8 slice_select_fusion
  24.2 77.9 %reduce-scatter.3.cloned.1.call-done = f32[192,256]{1,0:T(8,128)} async-done(((f32[3072,256]{1,0:T(8,128)}), f32[192,256]{1,0:T(8,128)}) %reduce-scatter.3.cloned.1.call-update) | async-done | bytes 196624 | tf_op jit(solution)/shard_map/reduce_scatter | solution.py:29
  102.2 0.0 all-reduce.5.cloned.1.call-start
  102.2 2.3 select_bitcast_fusion.1
  104.6 63.7 %all-gather.7.cloned.1.call-done = f32[3072,256]{1,0:T(8,128)} async-done(((f32[192,256]{1,0:T(8,128)}), f32[3072,256]{1,0:T(8,128)}) %all-gather.7.cloned.1.call-update) | async-done | bytes 3145744 | tf_op jit(solution)/shard_map/all_gather | solution.py:30
  168.2 1.3 convolution_subtract_fusion.5
  169.6 0.4 fusion.12
  169.9 1.3 convolution_subtract_fusion.4
  171.3 0.4 fusion.42
  171.7 1.3 convolution_subtract_fusion.3
  173.0 1.1 fusion.43
  174.1 0.0 all-reduce.7.cloned.1.call-start
  174.2 0.5 all-reduce.7.cloned.1.call-update
  174.7 0.0 reduce-scatter.5.cloned.1.call-start
  174.8 43.0 %all-gather.11.cloned.1.call-done = f32[2048,256]{1,0:T(8,128)} async-done(((f32[256,256]{1,0:T(8,128)}), f32[2048,256]{1,0:T(8,128)}) %all-gather.11.cloned.1.call-update) | async-done | bytes 2097168 | tf_op jit(solution)/shard_map/all_gather | solution.py:14
  217.9 4.6 fusion.16
  222.4 9.0 %all-reduce.7.cloned.1.call-done = f32[4,256,256]{2,1,0:T(8,128)} async-done(((f32[4,256,256]{2,1,0:T(8,128)}), f32[4,256,256]{2,1,0:T(8,128)}) %all-reduce.7.cloned.1.call-update) | async-done | bytes 1048592 | tf_op jit(solution)/shard_map/psum | solution.py:36
  231.4 6.1 %broadcast_select_fusion = (f32[12,1,256,256]{3,2,0,1:T(8,128)}, f32[12,1,256,256]{3,2,0,1:T(8,128)}) fusion(pred[]{:T(512)S(6)} %eq.80, f32[12,256,256]{2,1,0:T(8,128)S(1)} %fusion.16, f32[4,256,256]{2,1,0:T(8,128)} %all-reduce.7.cloned.1.call-done, f32[12,4,256,256]{3,2,0,1:T(8,128)} %fusion.2, pred[12]{0:T(512)(128)(4,1)S(1)} %get-tuple-element.13, ...), kind=kOutput, calls=%fused_computation.13 | convolution fusion | flops 2419064832 | bytes 15991809 | tf_op jit(solution)/shard_map/rab,cbe->rcae/dot_general | solution.py:55
  237.6 75.6 %reduce-scatter.5.cloned.1.call-done = f32[192,256]{1,0:T(8,128)} async-done(((f32[3072,256]{1,0:T(8,128)}), f32[192,256]{1,0:T(8,128)}) %reduce-scatter.5.cloned.1.call-update) | async-done | bytes 196624 | tf_op jit(solution)/shard_map/reduce_scatter | solution.py:29
  313.2 0.0 all-reduce.9.cloned.1.call-start
  313.4 2.7 fusion.7
  316.1 1.1 copy-done.2
  317.1 1.1 select_bitcast_fusion
  318.3 0.2 all-gather.13.cloned.1.call-start
  318.5 46.7 %all-gather.9.cloned.1.call-done = f32[3072,256]{1,0:T(8,128)} async-done(((f32[192,256]{1,0:T(8,128)}), f32[3072,256]{1,0:T(8,128)}) %all-gather.9.cloned.1.call-update) | async-done | bytes 3145744 | tf_op jit(solution)/shard_map/all_gather | solution.py:30
  365.2 1.3 convolution_subtract_fusion.2
  366.6 0.4 fusion.9
  367.0 1.3 convolution_subtract_fusion.1
  368.3 0.4 fusion.44
  368.7 1.3 convolution_subtract_fusion
  370.0 1.1 fusion.45
  371.2 0.0 all-reduce.11.cloned.1.call-start
  371.2 0.1 slice_compare_fusion
  371.3 0.1 slice_compare_fusion.2
  371.4 0.1 broadcast_and_fusion.1
  371.5 0.1 broadcast_and_fusion.3
  371.6 1.5 copy-done.1
  373.1 1.9 slice.75
  375.1 0.9 slice-done
  376.0 12.7 %fusion.3 = f32[11,3,256,256]{3,2,0,1:T(8,128)} fusion(f32[12,4,256,256]{3,2,0,1:T(8,128)} %fusion.2, f32[11,256,256]{2,1,0:T(8,128)S(1)} %slice-done, pred[11,3]{0,1:T(4,128)(4,1)S(1)} %get-tuple-element.8, pred[11,3]{0,1:T(4,128)(4,1)S(1)} %get-tuple-element.7, f32[4,256,256]{2,1,0:T(8,128)} %all-reduce.7.cloned.1.call-done), kind=kOutput, calls=%fused_computation.6 | convolution fusion | flops 6650265600 | bytes 23856128 | tf_op jit(solution)/shard_map/rab,cbe->rcae/dot_general | solution.py:55
  388.7 26.7 %all-gather.13.cloned.1.call-done = f32[2048,256]{1,0:T(8,128)} async-done(((f32[256,256]{1,0:T(8,128)}), f32[2048,256]{1,0:T(8,128)}) %all-gather.13.cloned.1.call-update) | async-done | bytes 2097168 | tf_op jit(solution)/shard_map/all_gather | solution.py:14
  415.4 6.4 %fusion.15 = f32[12,256,256]{2,1,0:T(8,128)} fusion(f32[12,256,256]{2,1,0:T(8,128)} %bitcast.91, f32[2048,256]{1,0:T(8,128)} %all-gather.13.cloned.1.call-done), kind=kOutput, calls=%fused_computation.33 | convolution fusion | flops 2415919104 | bytes 6553600 | tf_op jit(solution)/shard_map/rab,be->rae/dot_general | solution.py:84
  421.7 7.9 %all-reduce.11.cloned.1.call-done = f32[4,256,256]{2,1,0:T(8,128)} async-done(((f32[4,256,256]{2,1,0:T(8,128)}), f32[4,256,256]{2,1,0:T(8,128)}) %all-reduce.11.cloned.1.call-update) | async-done | bytes 1048592 | tf_op jit(solution)/shard_map/psum | solution.py:36
  429.7 18.2 %fusion.1 = f32[12,1,4,1,256,256]{5,4,0,2,3,1:T(8,128)} fusion(f32[11,3,256,256]{3,2,0,1:T(8,128)} %fusion.3, f32[11,1,256,256]{3,2,0,1:T(8,128)} %slice.75, f32[1,4,256,256]{3,2,0,1:T(8,128)S(1)} %copy-done.3, f32[12,256,256]{2,1,0:T(8,128)} %fusion.15, pred[12,4]{0,1:T(4,128)(4,1)S(1)} %get-tuple-element.6, pred[12,4]{0,1:T(4,128)(4,1)S(1)} %get-tuple-element.5, ...), kind=kOutput, calls=%fused_computation.3 | convolution fusion | flops 9679405056 | bytes 29360224 | tf_op jit(solution)/shard_map/rab,cbe->rcae/dot_general | solution.py:55
  447.9 10.8 %copy.10 = f32[12,1,4,1,256,256]{5,4,3,2,1,0:T(8,128)} copy(f32[12,1,4,1,256,256]{5,4,0,2,3,1:T(8,128)} %fusion.1) | data formatting | bytes 25165824 | tf_op jit(solution)/shard_map/broadcast_in_dim | solution.py:134
  (30 shorter events, 0.4 us)
Async XLA Ops:
  7.4 94.8 %reduce-scatter.3.cloned.1.call-start = ((), (), s32[]{:S(2)}) async-start(), calls=%async_computation.2 | async-start | bytes 3342336 | tf_op jit(solution)/shard_map/reduce_scatter | solution.py:29
  24.2 144.0 %all-gather.7.cloned.1.call-start = ((), (), s32[]{:S(2)}) async-start(), calls=%async_computation.3 | async-start | bytes 3342336 | tf_op jit(solution)/shard_map/all_gather | solution.py:30
  102.2 72.0 %all-reduce.5.cloned.1.call-start = ((), (), s32[]{:S(2)}) async-start(), calls=%async_computation.4 | async-start | bytes 2097152 | tf_op jit(solution)/shard_map/psum | solution.py:36
  104.5 113.3 %all-gather.11.cloned.1.call-start = ((), (), s32[]{:S(2)}) async-start(), calls=%async_computation.10 | async-start | bytes 2359296 | tf_op jit(solution)/shard_map/all_gather | solution.py:14
  174.1 57.3 %all-reduce.7.cloned.1.call-start = ((), (), s32[]{:S(2)}) async-start(), calls=%async_computation.5 | async-start | bytes 2097152 | tf_op jit(solution)/shard_map/psum | solution.py:36
  174.7 138.5 %reduce-scatter.5.cloned.1.call-start = ((), (), s32[]{:S(2)}) async-start(), calls=%async_computation.6 | async-start | bytes 3342336 | tf_op jit(solution)/shard_map/reduce_scatter | solution.py:29
  222.4 149.1 %copy-start = (f32[12,256,256]{2,1,0:T(8,128)}, f32[12,256,256]{2,1,0:T(8,128)S(1)}, u32[]{:S(2)}) copy-start(f32[12,256,256]{2,1,0:T(8,128)S(1)} %fusion.16) | copy-start | bytes 9437188
  237.5 127.7 %all-gather.9.cloned.1.call-start = ((), (), s32[]{:S(2)}) async-start(), calls=%async_computation.7 | async-start | bytes 3342336 | tf_op jit(solution)/shard_map/all_gather | solution.py:30
  313.2 61.8 %all-reduce.9.cloned.1.call-start = ((), (), s32[]{:S(2)}) async-start(), calls=%async_computation.8 | async-start | bytes 2097152 | tf_op jit(solution)/shard_map/psum | solution.py:36
  316.0 1.1 copy-start.2
  318.3 97.1 %all-gather.13.cloned.1.call-start = ((), (), s32[]{:S(2)}) async-start(), calls=%async_computation.11 | async-start | bytes 2359296 | tf_op jit(solution)/shard_map/all_gather | solution.py:14
  371.2 58.5 %all-reduce.11.cloned.1.call-start = ((), (), s32[]{:S(2)}) async-start(), calls=%async_computation.9 | async-start | bytes 2097152 | tf_op jit(solution)/shard_map/psum | solution.py:36
  371.2 1.9 copy-start.1
  373.1 2.9 slice-start
  415.4 14.3 %copy-start.3 = (f32[1,4,256,256]{3,2,0,1:T(8,128)S(1)}, f32[1,4,256,256]{3,2,0,1:T(8,128)}, u32[]{:S(2)}) copy-start(f32[1,4,256,256]{3,2,0,1:T(8,128)} %copy-done.2) | copy-start | bytes 3145732
Sparse Core Ops, SparseCore 0:
  24.3 77.7 reduce-scatter.2
  104.6 63.5 all-gather.6
  174.2 43.5 all-gather.10
  237.7 75.4 reduce-scatter.4
  315.5 49.6 all-gather.8
  371.3 44.0 all-gather.12
Sparse Core Ops, SparseCore 1:
  105.1 45.9 all-reduce.4
  177.1 54.3 all-reduce.6
  318.4 49.1 all-reduce.8
  375.1 54.5 all-reduce.10
where the time goes:
time: 467 us; the launch traced here: 466 us
  waiting for transfers between devices  351 us (75%)
  matrix products  62.3 us (13%)
  other arithmetic  20.5 us (4%)
  local copies, waits for them, and re-layouts  16.2 us (3%)
  between operations  15.4 us (3%)
    reduce_scatter x2, waiting for transfers between devices, spread(): own = lax.psum_scatter(padded, axis, scatter_dimension=0, tiled=True)  153 us
    all_gather x2, waiting for transfers between devices, spread(): lax.all_gather(own, axis, axis=0, tiled=True)[:len(lines)]  110 us
    all_gather x2, waiting for transfers between devices, picked(): lax.all_gather(value, axis)  69.7 us
    dot_general x4, matrix products, apply_panel(): jnp.einsum('rab,cbe->rcae', mult, upper, precision=lax.Precision.HIGHEST)  39.7 us
    psum x4, waiting for transfers between devices, broadcast_by_axis(): value = lax.psum(value, axis)  16.9 us
    add x1, other arithmetic, body(): blocks = blocks + diag[:, :, None, None] * eye  12.2 us
    dot_general x2, matrix products, factor_panel(): jnp.einsum('rab,be->rae', column, inverse, precision=lax.Precision.HIGHEST)  10.9 us
    broadcast_in_dim x1, local copies, waits for them, and re-layouts, body(): return blocks[:, None, :, None]  10.8 us
  transfers between devices with their start and end apart: 10, of which 8 were waited for; matrix products, arithmetic and copies ran while one was open for 9% of the time, Pallas kernels for 0%

commit v1 on v0

--- a/solution.py
+++ b/solution.py
@@ -33,7 +33,8 @@
 def broadcast_by_axis(value, axes, root):
     value = jnp.where(lax.axis_index(axes) == root, value, jnp.zeros_like(value))
     for axis in axes:
-        value = lax.psum(value, axis)
+        parts = lax.all_gather(value, axis)
+        value = jnp.sum(parts, axis=0)
     return value
 
 

time: 467 us -> 517 us (1.11)
  waiting for transfers between devices: 351 us -> 396 us
  other arithmetic: 20.5 us -> 32.3 us
    all_gather x0 -> x4, waiting for transfers between devices: none -> 69.7 us  [broadcast_by_axis(): parts = lax.all_gather(value, axis)]
    all_gather x2, waiting for transfers between devices: 110 us -> 93 us  [spread(): lax.all_gather(own, axis, axis=0, tiled=True)[:len(lines)]]
    psum x4 -> x0, waiting for transfers between devices: 16.9 us -> none  [broadcast_by_axis(): value = lax.psum(value, axis)]
    reduce_sum x0 -> x4, other arithmetic: none -> 12.9 us  [broadcast_by_axis(): value = jnp.sum(parts, axis=0)]
    all_gather x2, waiting for transfers between devices: 69.7 us -> 80.2 us  [picked(): lax.all_gather(value, axis)]
where the time goes in v1:
time: 517 us
  waiting for transfers between devices  396 us (77%)
  matrix products  58.6 us (11%)
  other arithmetic  32.3 us (6%)
  between operations  15.3 us (3%)
  local copies, waits for them, and re-layouts  14.3 us (3%)
    reduce_scatter x2, waiting for transfers between devices, spread(): own = lax.psum_scatter(padded, axis, scatter_dimension=0, tiled=True)  153 us
    all_gather x2, waiting for transfers between devices, spread(): lax.all_gather(own, axis, axis=0, tiled=True)[:len(lines)]  93 us
    all_gather x2, waiting for transfers between devices, picked(): lax.all_gather(value, axis)  80.2 us
    all_gather x4, waiting for transfers between devices, broadcast_by_axis(): parts = lax.all_gather(value, axis)  69.7 us
    dot_general x4, matrix products, apply_panel(): jnp.einsum('rab,cbe->rcae', mult, upper, precision=lax.Precision.HIGHEST)  38.7 us
    reduce_sum x4, other arithmetic, broadcast_by_axis(): value = jnp.sum(parts, axis=0)  12.9 us
    add x1, other arithmetic, body(): blocks = blocks + diag[:, :, None, None] * eye  12.2 us
    broadcast_in_dim x1, local copies, waits for them, and re-layouts, body(): return blocks[:, None, :, None]  10.8 us
  transfers between devices with their start and end apart: 10, of which 8 were waited for; matrix products, arithmetic and copies ran while one was open for 9% of the time, Pallas kernels for 0%

profile of v1, /device:TPU:0, one launch (start us, length us, event | category | flops | bytes accessed | tf_op | source)
XLA Modules:
  0.0 516.6 jit_solution(17868791792121970804)
XLA Ops:
  7.4 0.7 convert_element_type.19
  8.1 0.1 compare_select_fusion
  8.2 12.2 %fusion.2 = f32[12,4,256,256]{3,2,0,1:T(8,128)} fusion(f32[12,1,4,1,256,256]{5,4,3,2,1,0:T(8,128)} %param.2, f32[256,256]{1,0:T(8,128)S(1)} %fusion.18, f32[12,4]{0,1:T(4,128)S(1)} %compare_select_fusion, f32[12,4]{0,1:T(4,128)S(1)} %bitcast.95), kind=kLoop, calls=%fused_computation.5 | loop fusion | flops 9437184 | bytes 25428352 | tf_op jit(solution)/shard_map/add | solution.py:100
  20.4 3.8 slice_select_fusion
  24.2 0.0 all-gather.15.cloned.1.call-start
  24.3 2.3 slice_select_fusion.1
  26.6 0.0 all-gather.13.cloned.1.call-start
  26.6 77.9 %reduce-scatter.3.cloned.1.call-done = f32[192,256]{1,0:T(8,128)} async-done(((f32[3072,256]{1,0:T(8,128)}), f32[192,256]{1,0:T(8,128)}) %reduce-scatter.3.cloned.1.call-update) | async-done | bytes 196624 | tf_op jit(solution)/shard_map/reduce_scatter | solution.py:29
  104.6 2.8 reduce_sum.36
  107.5 0.0 all-gather.21.cloned.1.call-start
  107.5 46.6 %all-gather.13.cloned.1.call-done = f32[3072,256]{1,0:T(8,128)} async-done(((f32[192,256]{1,0:T(8,128)}), f32[3072,256]{1,0:T(8,128)}) %all-gather.13.cloned.1.call-update) | async-done | bytes 3145744 | tf_op jit(solution)/shard_map/all_gather | solution.py:30
  154.1 1.3 convolution_subtract_fusion.5
  155.4 0.4 fusion.12
  155.8 1.3 convolution_subtract_fusion.4
  157.1 0.4 fusion.42
  157.5 1.3 convolution_subtract_fusion.3
  158.9 1.1 fusion.43
  160.1 42.7 %all-gather.23.cloned.1.call-done = f32[16,256,256]{2,1,0:T(8,128)} async-done(((f32[4,256,256]{2,1,0:T(8,128)}), f32[16,256,256]{2,1,0:T(8,128)}) %all-gather.23.cloned.1.call-update) | async-done | bytes 4194320 | tf_op jit(solution)/shard_map/all_gather | solution.py:36
  202.8 3.6 reduce_sum.37
  206.4 40.2 %all-gather.21.cloned.1.call-done = f32[2048,256]{1,0:T(8,128)} async-done(((f32[256,256]{1,0:T(8,128)}), f32[2048,256]{1,0:T(8,128)}) %all-gather.21.cloned.1.call-update) | async-done | bytes 2097168 | tf_op jit(solution)/shard_map/all_gather | solution.py:14
  246.6 4.5 fusion.16
  251.1 7.3 %broadcast_select_fusion = (f32[12,1,256,256]{3,2,0,1:T(8,128)}, f32[12,1,256,256]{3,2,0,1:T(8,128)}) fusion(pred[]{:T(512)S(6)} %eq.80, f32[12,256,256]{2,1,0:T(8,128)S(1)} %fusion.16, f32[4,256,256]{2,1,0:T(8,128)} %reduce_sum.37, f32[12,4,256,256]{3,2,0,1:T(8,128)} %fusion.2, pred[12]{0:T(512)(128)(4,1)S(1)} %get-tuple-element.15, ...), kind=kOutput, calls=%fused_computation.13 | convolution fusion | flops 2419064832 | bytes 15991809 | tf_op jit(solution)/shard_map/rab,cbe->rcae/dot_general | solution.py:56
  258.4 0.0 all-gather.19.cloned.1.call-start
  258.6 4.1 broadcast_select_fusion.1
  262.7 74.7 %reduce-scatter.5.cloned.1.call-done = f32[192,256]{1,0:T(8,128)} async-done(((f32[3072,256]{1,0:T(8,128)}), f32[192,256]{1,0:T(8,128)}) %reduce-scatter.5.cloned.1.call-update) | async-done | bytes 196624 | tf_op jit(solution)/shard_map/reduce_scatter | solution.py:29
  337.5 0.2 all-gather.27.cloned.1.call-start
  337.8 2.9 reduce_sum.38
  340.6 0.0 all-gather.25.cloned.1.call-start
  340.7 46.4 %all-gather.17.cloned.1.call-done = f32[3072,256]{1,0:T(8,128)} async-done(((f32[192,256]{1,0:T(8,128)}), f32[3072,256]{1,0:T(8,128)}) %all-gather.17.cloned.1.call-update) | async-done | bytes 3145744 | tf_op jit(solution)/shard_map/all_gather | solution.py:30
  387.1 1.3 convolution_subtract_fusion.2
  388.4 0.4 fusion.9
  388.8 1.3 convolution_subtract_fusion.1
  390.1 0.4 fusion.44
  390.5 1.3 convolution_subtract_fusion
  391.9 1.1 fusion.45
  393.0 0.1 slice_compare_fusion
  393.1 0.1 slice_compare_fusion.2
  393.1 0.1 broadcast_and_fusion.1
  393.2 0.1 broadcast_and_fusion.3
  393.3 1.5 copy-done.1
  394.9 1.9 slice.75
  396.8 12.1 %fusion.3 = f32[11,3,256,256]{3,2,0,1:T(8,128)} fusion(f32[12,4,256,256]{3,2,0,1:T(8,128)} %fusion.2, f32[11,256,256]{2,1,0:T(8,128)S(1)} %slice-done, pred[11,3]{0,1:T(4,128)(4,1)S(1)} %get-tuple-element.8, pred[11,3]{0,1:T(4,128)(4,1)S(1)} %get-tuple-element.7, f32[4,256,256]{2,1,0:T(8,128)S(1)} %copy-done.2), kind=kOutput, calls=%fused_computation.6 | convolution fusion | flops 6650265600 | bytes 23856128 | tf_op jit(solution)/shard_map/rab,cbe->rcae/dot_general | solution.py:56
  408.9 26.9 %all-gather.27.cloned.1.call-done = f32[16,256,256]{2,1,0:T(8,128)} async-done(((f32[4,256,256]{2,1,0:T(8,128)}), f32[16,256,256]{2,1,0:T(8,128)}) %all-gather.27.cloned.1.call-update) | async-done | bytes 4194320 | tf_op jit(solution)/shard_map/all_gather | solution.py:36
  435.8 3.6 reduce_sum.39
  439.4 40.1 %all-gather.25.cloned.1.call-done = f32[2048,256]{1,0:T(8,128)} async-done(((f32[256,256]{1,0:T(8,128)}), f32[2048,256]{1,0:T(8,128)}) %all-gather.25.cloned.1.call-update) | async-done | bytes 2097168 | tf_op jit(solution)/shard_map/all_gather | solution.py:14
  479.4 3.7 fusion.15
  483.2 15.2 %fusion.1 = f32[12,1,4,1,256,256]{5,4,0,2,3,1:T(8,128)} fusion(f32[11,3,256,256]{3,2,0,1:T(8,128)} %fusion.3, f32[11,1,256,256]{3,2,0,1:T(8,128)S(1)} %copy-done.4, f32[1,4,256,256]{3,2,0,1:T(8,128)S(1)} %copy-done.5, f32[12,256,256]{2,1,0:T(8,128)S(1)} %fusion.15, pred[12,4]{0,1:T(4,128)(4,1)S(1)} %get-tuple-element.6, ...), kind=kOutput, calls=%fused_computation.3 | convolution fusion | flops 9679405056 | bytes 29360224 | tf_op jit(solution)/shard_map/rab,cbe->rcae/dot_general | solution.py:56
  498.4 10.8 %copy.24 = f32[12,1,4,1,256,256]{5,4,3,2,1,0:T(8,128)} copy(f32[12,1,4,1,256,256]{5,4,0,2,3,1:T(8,128)} %fusion.1) | data formatting | bytes 25165824 | tf_op jit(solution)/shard_map/broadcast_in_dim | solution.py:135
  (39 shorter events, 0.4 us)
Async XLA Ops:
  7.4 97.1 %reduce-scatter.3.cloned.1.call-start = ((), (), s32[]{:S(2)}) async-start(), calls=%async_computation.2 | async-start | bytes 3342336 | tf_op jit(solution)/shard_map/reduce_scatter | solution.py:29
  24.2 80.4 %all-gather.15.cloned.1.call-start = ((), (), s32[]{:S(2)}) async-start(), calls=%async_computation.4 | async-start | bytes 3145728 | tf_op jit(solution)/shard_map/all_gather | solution.py:36
  26.6 127.5 %all-gather.13.cloned.1.call-start = ((), (), s32[]{:S(2)}) async-start(), calls=%async_computation.3 | async-start | bytes 3342336 | tf_op jit(solution)/shard_map/all_gather | solution.py:30
  104.5 98.3 %all-gather.23.cloned.1.call-start = ((), (), s32[]{:S(2)}) async-start(), calls=%async_computation.9 | async-start | bytes 5242880 | tf_op jit(solution)/shard_map/all_gather | solution.py:36
  107.5 139.1 %all-gather.21.cloned.1.call-start = ((), (), s32[]{:S(2)}) async-start(), calls=%async_computation.8 | async-start | bytes 2359296 | tf_op jit(solution)/shard_map/all_gather | solution.py:14
  160.0 177.5 %reduce-scatter.5.cloned.1.call-start = ((), (), s32[]{:S(2)}) async-start(), calls=%async_computation.5 | async-start | bytes 3342336 | tf_op jit(solution)/shard_map/reduce_scatter | solution.py:29
  251.1 142.2 %copy-start = (f32[12,256,256]{2,1,0:T(8,128)}, f32[12,256,256]{2,1,0:T(8,128)S(1)}, u32[]{:S(2)}) copy-start(f32[12,256,256]{2,1,0:T(8,128)S(1)} %fusion.16) | copy-start | bytes 9437188
  258.4 79.3 %all-gather.19.cloned.1.call-start = ((), (), s32[]{:S(2)}) async-start(), calls=%async_computation.7 | async-start | bytes 3145728 | tf_op jit(solution)/shard_map/all_gather | solution.py:36
  262.7 124.4 %all-gather.17.cloned.1.call-start = ((), (), s32[]{:S(2)}) async-start(), calls=%async_computation.6 | async-start | bytes 3342336 | tf_op jit(solution)/shard_map/all_gather | solution.py:30
  337.5 98.3 %all-gather.27.cloned.1.call-start = ((), (), s32[]{:S(2)}) async-start(), calls=%async_computation.11 | async-start | bytes 5242880 | tf_op jit(solution)/shard_map/all_gather | solution.py:36
  340.6 138.8 %all-gather.25.cloned.1.call-start = ((), (), s32[]{:S(2)}) async-start(), calls=%async_computation.10 | async-start | bytes 2359296 | tf_op jit(solution)/shard_map/all_gather | solution.py:14
  393.0 1.9 copy-start.1
  393.3 3.5 slice-start
  393.3 3.5 copy-start.2
  408.9 70.5 %copy-start.3 = (f32[3072,256]{1,0:T(8,128)S(1)}, f32[3072,256]{1,0:T(8,128)}, u32[]{:S(2)}) copy-start(f32[3072,256]{1,0:T(8,128)} %all-gather.17.cloned.1.call-done) | copy-start | bytes 9437188
  479.4 3.7 copy-start.4
  479.4 3.7 copy-start.5
  479.4 3.8 copy-start.6
Sparse Core Ops, SparseCore 0:
  24.3 80.1 reduce-scatter.2
  258.5 78.8 reduce-scatter.4
Sparse Core Ops, SparseCore 1:
  26.6 38.2 all-gather.14
  104.6 49.4 all-gather.12
  155.6 47.1 all-gather.22
  204.5 42.1 all-gather.20
  262.8 35.1 all-gather.18
  337.6 49.4 all-gather.16
  388.6 47.1 all-gather.26
  437.3 42.1 all-gather.24
